TPU v7x, 32 devices: a whole 2x2x4 slice. The times are simulated.
32 devices in a mesh: gx: 8 (over y, x, core), gy: 4 (over z).
Axes of the slice: x: 2, y: 2, z: 4, core: 2. Of those that a mesh axis runs over, the one named last changes fastest.
Arguments:
- features: bfloat16 [64, 64, 32, 128], P(None, 'gx', 'gy'), may hold values from -6 to 6
- cotangent: bfloat16 [64, 64, 32, 128], P(None, 'gx', 'gy'), may hold values from -6 to 6
- block_mask: int32 [8, 4, 16], P('gx', 'gy'), may hold values from 0 to 1, as said below
- kernel_one: bfloat16 [3, 3, 3, 64, 64], replicated, may hold values from -0.15625 to 0.15625
- kernel_two: bfloat16 [3, 3, 3, 64, 64], replicated, may hold values from -0.15625 to 0.15625
Outputs:
- grad_features: bfloat16 [64, 64, 32, 128], P(None, 'gx', 'gy')
- grad_one: float32 [3, 3, 3, 64, 64], replicated
- grad_two: float32 [3, 3, 3, 64, 64], replicated
Inputs may be any that keep to these rules, and one draw needn't show every extreme that they name: `block_mask`: 1 marks an active block of 8 x 8 x 8 cells, 0 an empty one.
All inputs are finite; a program needn't handle non-finite values.
Results may differ from a plain program's by a relative error of at most 0.0032.
Values may be sent and summed in bfloat16 or wider, within the bound.
A program may use at most 192 MiB of HBM per device.

v0:
```python
import math

import jax
import jax.numpy as jnp
from jax import lax
from jax.sharding import PartitionSpec as P

BS = 8


def padded_2(cells, sides, width):
    for axis, dim in sides:
        count = lax.axis_size(axis)
        ends = count - 1
        head = lax.slice_in_dim(cells, 0, width, axis=dim)
        tail = lax.slice_in_dim(cells, cells.shape[dim] - width, cells.shape[dim], axis=dim)
        cells = jnp.concatenate(
            [
                lax.ppermute(tail, axis, [(i, (i + 1) % count) for i in range(ends)]),
                cells,
                lax.ppermute(head, axis, [((i + 1) % count, i) for i in range(ends)]),
            ],
            axis=dim,
        )
    return cells


def upsample(block_mask):
    nbx, nby, nbz = block_mask.shape
    wide = jnp.broadcast_to(block_mask[:, None, :, None, :, None], (nbx, BS, nby, BS, nbz, BS))
    return wide.reshape(nbx * BS, nby * BS, nbz * BS)


def flip_kernel(kernel):
    return jnp.transpose(jnp.flip(kernel, (0, 1, 2)), (0, 1, 2, 4, 3))


def silu_slope(value):
    sig = jax.nn.sigmoid(value)
    return sig * (1.0 + value * (1.0 - sig))


def stack_depth(source):
    depth = source.shape[-1]
    padded = jnp.pad(source, ((0, 0), (0, 0), (0, 0), (1, 1)))
    return jnp.concatenate(
        [padded[..., 0:depth], padded[..., 1 : depth + 1], padded[..., 2 : depth + 2]], 0
    )


def stack_reverse(source):
    depth = source.shape[-1]
    padded = jnp.pad(source, ((0, 0), (0, 0), (0, 0), (1, 1)))
    return jnp.concatenate(
        [padded[..., 2 : depth + 2], padded[..., 1 : depth + 1], padded[..., 0:depth]], 0
    )


def conv_pad(source, kernel, size_x, size_y):
    stacked = stack_depth(source)
    folded = kernel.reshape(3, 3, 3 * kernel.shape[3], kernel.shape[4])
    total = None
    for row_off in range(3):
        for col_off in range(3):
            window = stacked[:, row_off : row_off + size_x, col_off : col_off + size_y]
            term = jnp.einsum(
                "co,cxyz->oxyz",
                folded[row_off, col_off],
                window,
                preferred_element_type=jnp.float32,
            )
            total = term if total is None else total + term
    return total


def grad_forward(source, grad, size_x, size_y):
    stacked = stack_depth(source)
    pieces = []
    for row_off in range(3):
        for col_off in range(3):
            window = stacked[:, row_off : row_off + size_x, col_off : col_off + size_y]
            pieces.append(
                jnp.einsum("cxyz,oxyz->co", window, grad, preferred_element_type=jnp.float32)
            )
    return jnp.stack(pieces, 0).reshape(3, 3, 3, source.shape[0], grad.shape[0])


def grad_backward(activ, grad_pad, size_x, size_y):
    stacked = stack_reverse(grad_pad)
    pieces = []
    for row_off in range(3):
        for col_off in range(3):
            start_x = 2 - row_off
            start_y = 2 - col_off
            window = stacked[:, start_x : start_x + size_x, start_y : start_y + size_y]
            block = jnp.einsum("cxyz,kxyz->ck", activ, window, preferred_element_type=jnp.float32)
            block = block.reshape(activ.shape[0], 3, grad_pad.shape[0])
            pieces.append(jnp.transpose(block, (1, 0, 2)))
    return jnp.stack(pieces, 0).reshape(3, 3, 3, activ.shape[0], grad_pad.shape[0])


def shards(features, cotangent, block_mask, kernel_one, kernel_two):
    chans, tile_x, tile_y, tile_z = features.shape
    cell = upsample(block_mask).astype(jnp.bfloat16)[None]
    cell_f = cell.astype(jnp.float32)
    masked_in = features * cell
    masked_grad = cotangent * cell
    flip_one = flip_kernel(kernel_one)
    flip_two = flip_kernel(kernel_two)
    cells_all = tile_x * tile_y * tile_z * lax.axis_size("gx") * lax.axis_size("gy")
    scale = 1.0 / math.sqrt(cells_all)
    in_pad, grad_pad = (
        padded_2(masked_in, (("gx", 1), ("gy", 2)), 1),
        padded_2(masked_grad, (("gx", 1), ("gy", 2)), 1),
    )
    pre_act = conv_pad(in_pad, kernel_one, tile_x, tile_y)
    activ = (cell_f * jax.nn.silu(pre_act)).astype(jnp.bfloat16)
    partial_two = grad_backward(activ, grad_pad, tile_x, tile_y)
    summed_two = partial_two
    act_grad = conv_pad(grad_pad, flip_two, tile_x, tile_y)
    pre_grad = (cell_f * silu_slope(pre_act) * act_grad).astype(jnp.bfloat16)
    hidden_pad = padded_2(pre_grad, (("gx", 1), ("gy", 2)), 1)
    partial_one = grad_forward(in_pad, pre_grad, tile_x, tile_y)
    branch = conv_pad(hidden_pad, flip_one, tile_x, tile_y)
    grad_features = (cell_f * (cotangent.astype(jnp.float32) + branch)).astype(jnp.bfloat16)
    summed_one, summed_two = lax.psum((partial_one, summed_two), ("gx", "gy"))
    return (grad_features, summed_one * scale, summed_two * scale)


def solution(mesh):
    placed = (P(None, "gx", "gy", None), P(None, "gx", "gy", None), P("gx", "gy", None), P(), P())
    return jax.shard_map(
        shards,
        mesh=mesh,
        in_specs=placed,
        out_specs=(P(None, "gx", "gy", None), P(), P()),
        check_vma=False,
    )
```

profile of v0, /device:TPU:0, one launch (start us, length us, event | category | flops | bytes accessed | tf_op | source)
XLA Modules:
  0.0 261.0 jit_solution(13861000235684289690)
XLA Ops:
  8.1 3.3 %copy_multiply_fusion.1 = (bf16[64,8,8,128]{3,0,2,1:T(8,128)(2,1)S(1)}, bf16[64,8,8,128]{3,0,2,1:T(8,128)(2,1)S(1)}) fusion(bf16[64,8,8,128]{3,2,1,0:T(8,128)(2,1)} %param.6, bf16[128]{0:T(256)(128)(2,1)S(1)} %convert_element_type.40, bf16[64,8,8,128]{3,2,1,0:T(8,128)(2,1)} %param.5), kind=kLoop, calls=%fused_computation.141 | loop fusion | flops 1048576 | bytes 4194560 | tf_op jit(solution)/shard_map/mul | solution.py:107
  11.5 2.4 collective-permute-start
  13.8 1.3 collective-permute-start.1
  15.9 5.3 %collective-permute-start.4 = (bf16[64,1,8,128]{3,0,2,1:T(8,128)(2,1)}, bf16[64,1,8,128]{3,0,2,1:T(8,128)(2,1)S(1)}, u32[]{:S(2)}, u32[]{:S(2)}) collective-permute-start(bf16[64,1,8,128]{3,0,2,1:T(8,128)(2,1)} %get-tuple-element.27), channel_id=1, source_target_pairs={{0,4},{4,8},{8,12},{12,16},{16,20},{20,24},{24,28},{1,5},{5,9},{9,... | collective-permute-start | bytes 393224 | tf_op jit(solution)/shard_map/ppermute | solution.py:19
  21.1 1.3 collective-permute-start.5
  22.5 0.8 pad_maximum_fusion.13
  23.3 4.1 %collective-permute-start.2 = (bf16[64,10,1,128]{3,0,2,1:T(8,128)(2,1)}, bf16[64,10,1,128]{3,0,2,1:T(8,128)(2,1)}, u32[]{:S(2)}, u32[]{:S(2)}) collective-permute-start(bf16[64,10,1,128]{3,0,2,1:T(8,128)(2,1)} %get-tuple-element.23), channel_id=1, source_target_pairs={{0,1},{1,2},{2,3},{4,5},{5,6},{6,7},{8,9},{9,10},{10,11},{12,13},{... | collective-permute-start | bytes 491528 | tf_op jit(solution)/shard_map/ppermute | solution.py:19
  27.4 1.3 collective-permute-start.3
  29.3 1.0 copy.29
  30.3 1.0 copy.39
  31.2 0.8 pad_maximum_fusion.10
  32.0 4.6 %collective-permute-start.6 = (bf16[64,10,1,128]{3,0,2,1:T(8,128)(2,1)S(1)}, bf16[64,10,1,128]{3,0,2,1:T(8,128)(2,1)S(1)}, u32[]{:S(2)}, u32[]{:S(2)}) collective-permute-start(bf16[64,10,1,128]{3,0,2,1:T(8,128)(2,1)S(1)} %get-tuple-element.21), channel_id=1, source_target_pairs={{0,1},{1,2},{2,3},{4,5},{5,6},{6,7},{8,9},{9,10},{10,11},{12,13},{... | collective-permute-start | bytes 491528 | tf_op jit(solution)/shard_map/ppermute | solution.py:19
  36.6 1.5 collective-permute-start.7
  38.1 4.0 %fusion.15 = bf16[64,10,10,130]{3,0,2,1:T(8,128)(2,1)S(1)} fusion(bf16[64,10,1,128]{3,0,2,1:T(8,128)(2,1)} %collective-permute-done.3, bf16[64,10,1,128]{3,0,2,1:T(8,128)(2,1)} %collective-permute-done.2, bf16[64,1,8,128]{3,0,2,1:T(8,128)(2,1)} %copy-done.6, bf16[64,8,8,128]{3,0,2,1:T(8,128)(2,1)S(1)} %get-tuple-element.32, bf16[64,1,8,128]{3,0,2,1:T(8,128)(2,1)} %copy-done.4), kind=kLoop, calls=%fused_computation.24 | loop fusion | flops 14976000 | bytes 3302400 | tf_op jit(solution)/shard_map/concatenate | solution.py:17
  42.1 0.9 fusion.124
  43.1 4.9 %pad_maximum_fusion = bf16[192,10,10,128]{3,0,2,1:T(8,128)(2,1)S(1)} fusion(bf16[64,10,10,128]{3,0,2,1:T(8,128)(2,1)S(1)} %get-tuple-element.18, bf16[64,10,1,128]{3,0,2,1:T(8,128)(2,1)} %collective-permute-done.3, bf16[64,1,8,128]{3,0,2,1:T(8,128)(2,1)S(1)} %copy-done.7, bf16[64,8,8,128]{3,0,2,1:T(8,128)(2,1)S(1)} %get-tuple-element.32, ...), kind=kLoop, calls=%fused_computation.3 | loop fusion | flops 34406400 | bytes 9830400 | tf_op jit(solution)/shard_map/concatenate | solution.py:46
  53.1 0.7 fusion.94
  53.9 3.9 %fusion.19 = bf16[64,10,10,130]{3,0,2,1:T(8,128)(2,1)S(1)} fusion(bf16[64,10,1,128]{3,0,2,1:T(8,128)(2,1)S(1)} %collective-permute-done.7, bf16[64,10,1,128]{3,0,2,1:T(8,128)(2,1)S(1)} %collective-permute-done.6, bf16[64,1,8,128]{3,0,2,1:T(8,128)(2,1)} %collective-permute-done.5, bf16[64,8,8,128]{3,0,2,1:T(8,128)(2,1)S(1)} %get-tuple-element.31, ...), kind=kLoop, calls=%fused_computation.28 | loop fusion | flops 14976000 | bytes 3302400 | tf_op jit(solution)/shard_map/concatenate | solution.py:17
  57.9 2.1 fusion.123
  60.0 1.7 fusion.106
  61.7 5.5 %pad_maximum_fusion.4 = (bf16[192,10,10,128]{3,0,2,1:T(8,128)(2,1)S(1)}, bf16[192,10,10,128]{3,0,2,1:T(8,128)(2,1)S(1)}) fusion(bf16[64,10,10,128]{3,0,2,1:T(8,128)(2,1)S(1)} %get-tuple-element.15, bf16[64,10,10,128]{3,0,2,1:T(8,128)(2,1)} %get-tuple-element.16, bf16[64,10,1,128]{3,0,2,1:T(8,128)(2,1)S(1)} %collective-permute-done.7, ...), kind=kLoop, calls=%fused_computation.7 | loop fusion | flops 46694400 | bytes 14745600 | tf_op jit(solution)/shard_map/concatenate | solution.py:54
  67.2 1.0 fusion.24
  68.1 1.0 fusion.26
  69.1 1.0 fusion.28
  70.1 1.0 fusion.30
  71.0 1.0 fusion.32
  72.0 1.0 fusion.34
  73.0 1.0 fusion.36
  73.9 1.0 fusion.38
  74.9 1.6 fusion.40
  77.3 0.7 fusion.64
  78.0 0.7 fusion.66
  78.7 0.7 fusion.68
  79.5 0.7 fusion.70
  80.2 0.7 fusion.72
  81.0 0.7 fusion.74
  81.7 2.1 fusion.76
  83.8 3.5 %fusion.98 = bf16[64,8,8,128]{3,0,2,1:T(8,128)(2,1)S(1)} fusion(f32[8,8,128,64]{2,3,1,0:T(8,128)S(1)} %get-tuple-element.34, f32[8,8,128,64]{2,3,1,0:T(8,128)S(1)} %fusion.62, f32[8,8,128,64]{2,3,1,0:T(8,128)S(1)} %fusion.64, f32[8,8,128,64]{2,3,1,0:T(8,128)S(1)} %fusion.66, f32[8,8,128,64]{2,3,1,0:T(8,128)S(1)} %fusion.68, ...), kind=kOutput, calls=%fused_computation.109 | convolution fusion | flops 210763776 | bytes 23118336 | tf_op jit(solution)/shard_map/co,cxyz->oxyz/dot_general | solution.py:66
  87.4 1.1 fusion.115
  88.5 3.4 %collective-permute-start.8 = (bf16[64,1,8,128]{3,0,2,1:T(8,128)(2,1)S(1)}, bf16[64,1,8,128]{3,0,2,1:T(8,128)(2,1)S(1)}, u32[]{:S(2)}, u32[]{:S(2)}) collective-permute-start(bf16[64,1,8,128]{3,0,2,1:T(8,128)(2,1)S(1)} %get-tuple-element.25), channel_id=1, source_target_pairs={{0,4},{4,8},{8,12},{12,16},{16,20},{20,24},{24,28},{1,5},{5,9},{9,... | collective-permute-start | bytes 393224 | tf_op jit(solution)/shard_map/ppermute | solution.py:19
  92.0 1.3 collective-permute-start.9
  93.3 1.1 fusion.114
  94.4 1.1 fusion.113
  95.5 1.1 fusion.112
  96.6 1.1 fusion.111
  97.7 1.1 fusion.110
  98.8 1.1 fusion.109
  99.9 1.1 fusion.108
  101.0 1.1 fusion.107
  102.3 4.3 %collective-permute-start.10 = (bf16[64,10,1,128]{3,0,2,1:T(8,128)(2,1)S(1)}, bf16[64,10,1,128]{3,0,2,1:T(8,128)(2,1)S(1)}, u32[]{:S(2)}, u32[]{:S(2)}) collective-permute-start(bf16[64,10,1,128]{3,0,2,1:T(8,128)(2,1)S(1)} %get-tuple-element.19), channel_id=1, source_target_pairs={{0,1},{1,2},{2,3},{4,5},{5,6},{6,7},{8,9},{9,10},{10,11},{12,13},{... | collective-permute-start | bytes 491528 | tf_op jit(solution)/shard_map/ppermute | solution.py:19
  106.6 1.5 collective-permute-start.11
  108.2 1.2 copy.59
  109.4 1.2 copy.49
  110.6 3.2 %collective-permute-done.11 = bf16[64,10,1,128]{3,0,2,1:T(8,128)(2,1)S(1)} collective-permute-done((bf16[64,10,1,128]{3,0,2,1:T(8,128)(2,1)S(1)}, bf16[64,10,1,128]{3,0,2,1:T(8,128)(2,1)S(1)}, u32[]{:S(2)}, u32[]{:S(2)}) %collective-permute-start.11) | collective-permute-done | bytes 163872 | tf_op jit(solution)/shard_map/ppermute | solution.py:21
  113.8 3.1 %select_maximum_fusion = bf16[64,10,10,130]{3,0,2,1:T(8,128)(2,1)S(1)} fusion(bf16[64,10,1,128]{3,0,2,1:T(8,128)(2,1)S(1)} %collective-permute-done.11, bf16[64,10,1,128]{3,0,2,1:T(8,128)(2,1)S(1)} %collective-permute-done.10, bf16[64,1,8,128]{3,0,2,1:T(8,128)(2,1)S(1)} %collective-permute-done.9, bf16[64,8,8,128]{3,0,2,1:T(8,128)(2,1)S(1)} %fusion.98, ...), kind=kLoop, calls=%fused_computation.8 | loop fusion | flops 14976000 | bytes 3302400 | tf_op jit(solution)/shard_map/concatenate | solution.py:17
  116.9 0.9 fusion.122
  117.8 4.3 %pad_maximum_fusion.3 = bf16[192,10,10,128]{3,0,2,1:T(8,128)(2,1)S(1)} fusion(bf16[64,10,10,128]{3,0,2,1:T(8,128)(2,1)S(1)} %get-tuple-element.14, bf16[64,10,1,128]{3,0,2,1:T(8,128)(2,1)S(1)} %collective-permute-done.11, bf16[64,1,8,128]{3,0,2,1:T(8,128)(2,1)S(1)} %collective-permute-done.9, bf16[64,8,8,128]{3,0,2,1:T(8,128)(2,1)S(1)} %fusion.98, ...), kind=kLoop, calls=%fused_computation.6 | loop fusion | flops 34406400 | bytes 9830400 | tf_op jit(solution)/shard_map/concatenate | solution.py:46
  124.4 0.7 fusion.50
  125.1 0.7 fusion.52
  125.8 0.7 fusion.54
  128.6 2.2 fusion.97
  130.8 1.6 copy.60
  132.5 118.3 %all-reduce.6.cloned.1.call-done = (f32[3,3,3,64,64]{4,3,2,1,0:T(8,128)}, f32[3,3,3,64,64]{4,3,2,1,0:T(8,128)}) async-done(((f32[3,3,3,64,64]{4,3,2,1,0:T(8,128)}, f32[3,3,3,64,64]{4,3,2,1,0:T(8,128)}), (f32[3,3,3,64,64]{4,3,2,1,0:T(8,128)}, f32[3,3,3,64,64]{4,3,2,1,0:T(8,128)})) %all-reduce.6.cloned.1.call-update) | async-done | bytes 884752 | tf_op jit(solution)/shard_map/psum | solution.py:126
  250.8 2.9 %broadcast_multiply_fusion = (f32[3,3,3,64,64]{4,3,2,1,0:T(8,128)}, f32[3,3,3,64,64]{4,3,2,1,0:T(8,128)}) fusion(f32[3,3,3,64,64]{4,3,2,1,0:T(8,128)} %get-tuple-element.10, f32[3,3,3,64,64]{4,3,2,1,0:T(8,128)} %get-tuple-element.9), kind=kLoop, calls=%fused_computation.142 | loop fusion | flops 221184 | bytes 1769472 | tf_op jit(solution)/shard_map/mul | solution.py:127
  (71 shorter events, 12.6 us)
Async XLA Ops:
  7.2 15.3 %copy-start.8 = (bf16[3,3,3,64,64]{4,3,2,1,0:T(8,128)(2,1)S(1)}, bf16[3,3,3,64,64]{4,3,2,1,0:T(8,128)(2,1)}, u32[]{:S(2)}) copy-start(bf16[3,3,3,64,64]{4,3,2,1,0:T(8,128)(2,1)} %param.9) | copy-start | bytes 663556
  7.2 243.6 %all-reduce.6.cloned.1.call-start = ((), (), s32[]{:S(2)}) async-start(), calls=%async_computation | async-start | bytes 3538944 | tf_op jit(solution)/shard_map/psum | solution.py:126
  8.1 7.8 %copy-start.11 = (bf16[128]{0:T(256)(128)(2,1)}, bf16[128]{0:T(256)(128)(2,1)S(1)}, u32[]{:S(2)}) copy-start(bf16[128]{0:T(256)(128)(2,1)S(1)} %convert_element_type.40) | copy-start | bytes 772
  8.1 20.6 %copy-start.1 = (bf16[3,3,3,64,64]{4,3,2,1,0:T(8,128)(2,1)S(1)}, bf16[3,3,3,64,64]{4,3,2,1,0:T(8,128)(2,1)}, u32[]{:S(2)}) copy-start(bf16[3,3,3,64,64]{4,3,2,1,0:T(8,128)(2,1)} %param.8) | copy-start | bytes 663556
  11.5 11.0 %collective-permute-start = (bf16[64,1,8,128]{3,0,2,1:T(8,128)(2,1)S(1)}, bf16[64,1,8,128]{3,0,2,1:T(8,128)(2,1)S(1)}, u32[]{:S(2)}, u32[]{:S(2)}) collective-permute-start(bf16[64,1,8,128]{3,0,2,1:T(8,128)(2,1)S(1)} %get-tuple-element.29), channel_id=1, source_target_pairs={{0,4},{4,8},{8,12},{12,16},{16,20},{20,24},{24,28},{1,5},{5,9},{9,... | collective-permute-start | bytes 393224 | tf_op jit(solution)/shard_map/ppermute | solution.py:19
  13.8 8.7 %collective-permute-start.1 = (bf16[64,1,8,128]{3,0,2,1:T(8,128)(2,1)S(1)}, bf16[64,1,8,128]{3,0,2,1:T(8,128)(2,1)S(1)}, u32[]{:S(2)}, u32[]{:S(2)}) collective-permute-start(bf16[64,1,8,128]{3,0,2,1:T(8,128)(2,1)S(1)} %get-tuple-element.30), channel_id=1, source_target_pairs={{4,0},{8,4},{12,8},{16,12},{20,16},{24,20},{28,24},{5,1},{9,5},{13... | collective-permute-start | bytes 393224 | tf_op jit(solution)/shard_map/ppermute | solution.py:21
  15.9 12.9 %copy-start.12 = (bf16[128]{0:T(256)(128)(2,1)S(1)}, bf16[128]{0:T(256)(128)(2,1)}, u32[]{:S(2)}) copy-start(bf16[128]{0:T(256)(128)(2,1)} %copy-done.11) | copy-start | bytes 772
  15.9 15.4 %collective-permute-start.4 = (bf16[64,1,8,128]{3,0,2,1:T(8,128)(2,1)}, bf16[64,1,8,128]{3,0,2,1:T(8,128)(2,1)S(1)}, u32[]{:S(2)}, u32[]{:S(2)}) collective-permute-start(bf16[64,1,8,128]{3,0,2,1:T(8,128)(2,1)} %get-tuple-element.27), channel_id=1, source_target_pairs={{0,4},{4,8},{8,12},{12,16},{16,20},{20,24},{24,28},{1,5},{5,9},{9,... | collective-permute-start | bytes 393224 | tf_op jit(solution)/shard_map/ppermute | solution.py:19
  21.1 10.1 %collective-permute-start.5 = (bf16[64,1,8,128]{3,0,2,1:T(8,128)(2,1)}, bf16[64,1,8,128]{3,0,2,1:T(8,128)(2,1)}, u32[]{:S(2)}, u32[]{:S(2)}) collective-permute-start(bf16[64,1,8,128]{3,0,2,1:T(8,128)(2,1)} %get-tuple-element.28), channel_id=1, source_target_pairs={{4,0},{8,4},{12,8},{16,12},{20,16},{24,20},{28,24},{5,1},{9,5},{13... | collective-permute-start | bytes 393224 | tf_op jit(solution)/shard_map/ppermute | solution.py:21
  22.5 4.9 %copy-start.4 = (bf16[64,1,8,128]{3,0,2,1:T(8,128)(2,1)}, bf16[64,1,8,128]{3,0,2,1:T(8,128)(2,1)S(1)}, u32[]{:S(2)}) copy-start(bf16[64,1,8,128]{3,0,2,1:T(8,128)(2,1)S(1)} %collective-permute-done) | copy-start | bytes 393220
  22.5 6.2 %copy-start.6 = (bf16[64,1,8,128]{3,0,2,1:T(8,128)(2,1)}, bf16[64,1,8,128]{3,0,2,1:T(8,128)(2,1)S(1)}, u32[]{:S(2)}) copy-start(bf16[64,1,8,128]{3,0,2,1:T(8,128)(2,1)S(1)} %collective-permute-done.1) | copy-start | bytes 393220
  23.3 14.8 %collective-permute-start.2 = (bf16[64,10,1,128]{3,0,2,1:T(8,128)(2,1)}, bf16[64,10,1,128]{3,0,2,1:T(8,128)(2,1)}, u32[]{:S(2)}, u32[]{:S(2)}) collective-permute-start(bf16[64,10,1,128]{3,0,2,1:T(8,128)(2,1)} %get-tuple-element.23), channel_id=1, source_target_pairs={{0,1},{1,2},{2,3},{4,5},{5,6},{6,7},{8,9},{9,10},{10,11},{12,13},{... | collective-permute-start | bytes 491528 | tf_op jit(solution)/shard_map/ppermute | solution.py:19
  27.4 10.6 %collective-permute-start.3 = (bf16[64,10,1,128]{3,0,2,1:T(8,128)(2,1)}, bf16[64,10,1,128]{3,0,2,1:T(8,128)(2,1)}, u32[]{:S(2)}, u32[]{:S(2)}) collective-permute-start(bf16[64,10,1,128]{3,0,2,1:T(8,128)(2,1)} %get-tuple-element.24), channel_id=1, source_target_pairs={{1,0},{2,1},{3,2},{5,4},{6,5},{7,6},{9,8},{10,9},{11,10},{13,12},{... | collective-permute-start | bytes 491528 | tf_op jit(solution)/shard_map/ppermute | solution.py:21
  32.0 21.9 %collective-permute-start.6 = (bf16[64,10,1,128]{3,0,2,1:T(8,128)(2,1)S(1)}, bf16[64,10,1,128]{3,0,2,1:T(8,128)(2,1)S(1)}, u32[]{:S(2)}, u32[]{:S(2)}) collective-permute-start(bf16[64,10,1,128]{3,0,2,1:T(8,128)(2,1)S(1)} %get-tuple-element.21), channel_id=1, source_target_pairs={{0,1},{1,2},{2,3},{4,5},{5,6},{6,7},{8,9},{9,10},{10,11},{12,13},{... | collective-permute-start | bytes 491528 | tf_op jit(solution)/shard_map/ppermute | solution.py:19
  36.6 17.3 %collective-permute-start.7 = (bf16[64,10,1,128]{3,0,2,1:T(8,128)(2,1)S(1)}, bf16[64,10,1,128]{3,0,2,1:T(8,128)(2,1)S(1)}, u32[]{:S(2)}, u32[]{:S(2)}) collective-permute-start(bf16[64,10,1,128]{3,0,2,1:T(8,128)(2,1)S(1)} %get-tuple-element.22), channel_id=1, source_target_pairs={{1,0},{2,1},{3,2},{5,4},{6,5},{7,6},{9,8},{10,9},{11,10},{13,12},{... | collective-permute-start | bytes 491528 | tf_op jit(solution)/shard_map/ppermute | solution.py:21
  42.1 0.9 copy-start.5
  42.1 1.0 copy-start.7
  57.8 2.1 copy-start.10
  74.9 1.6 copy-start.3
  87.3 1.2 copy-start.9
  88.5 13.7 %collective-permute-start.8 = (bf16[64,1,8,128]{3,0,2,1:T(8,128)(2,1)S(1)}, bf16[64,1,8,128]{3,0,2,1:T(8,128)(2,1)S(1)}, u32[]{:S(2)}, u32[]{:S(2)}) collective-permute-start(bf16[64,1,8,128]{3,0,2,1:T(8,128)(2,1)S(1)} %get-tuple-element.25), channel_id=1, source_target_pairs={{0,4},{4,8},{8,12},{12,16},{16,20},{20,24},{24,28},{1,5},{5,9},{9,... | collective-permute-start | bytes 393224 | tf_op jit(solution)/shard_map/ppermute | solution.py:19
  92.0 10.3 %collective-permute-start.9 = (bf16[64,1,8,128]{3,0,2,1:T(8,128)(2,1)S(1)}, bf16[64,1,8,128]{3,0,2,1:T(8,128)(2,1)S(1)}, u32[]{:S(2)}, u32[]{:S(2)}) collective-permute-start(bf16[64,1,8,128]{3,0,2,1:T(8,128)(2,1)S(1)} %get-tuple-element.26), channel_id=1, source_target_pairs={{4,0},{8,4},{12,8},{16,12},{20,16},{24,20},{28,24},{5,1},{9,5},{13... | collective-permute-start | bytes 393224 | tf_op jit(solution)/shard_map/ppermute | solution.py:21
  102.3 8.3 %collective-permute-start.10 = (bf16[64,10,1,128]{3,0,2,1:T(8,128)(2,1)S(1)}, bf16[64,10,1,128]{3,0,2,1:T(8,128)(2,1)S(1)}, u32[]{:S(2)}, u32[]{:S(2)}) collective-permute-start(bf16[64,10,1,128]{3,0,2,1:T(8,128)(2,1)S(1)} %get-tuple-element.19), channel_id=1, source_target_pairs={{0,1},{1,2},{2,3},{4,5},{5,6},{6,7},{8,9},{9,10},{10,11},{12,13},{... | collective-permute-start | bytes 491528 | tf_op jit(solution)/shard_map/ppermute | solution.py:19
  106.6 7.2 %collective-permute-start.11 = (bf16[64,10,1,128]{3,0,2,1:T(8,128)(2,1)S(1)}, bf16[64,10,1,128]{3,0,2,1:T(8,128)(2,1)S(1)}, u32[]{:S(2)}, u32[]{:S(2)}) collective-permute-start(bf16[64,10,1,128]{3,0,2,1:T(8,128)(2,1)S(1)} %get-tuple-element.20), channel_id=1, source_target_pairs={{1,0},{2,1},{3,2},{5,4},{6,5},{7,6},{9,8},{10,9},{11,10},{13,12},{... | collective-permute-start | bytes 491528 | tf_op jit(solution)/shard_map/ppermute | solution.py:21
  117.8 4.4 %copy-start.2 = (bf16[3,3,3,64,64]{4,3,2,1,0:T(8,128)(2,1)S(1)}, bf16[3,3,3,64,64]{4,3,2,1,0:T(8,128)(2,1)}, u32[]{:S(2)}) copy-start(bf16[3,3,3,64,64]{4,3,2,1,0:T(8,128)(2,1)} %copy.39) | copy-start | bytes 663556
  127.3 1.2 copy-start
Sparse Core Ops, SparseCore 0:
  110.8 139.9 all-reduce.5
where the time goes:
time: 265 us; the launch traced here: 261 us
  waiting for transfers between devices  122 us (46%)
  matrix products  45.8 us (17%)
  other arithmetic  34.7 us (13%)
  starting transfers between devices  32.2 us (12%)
  between operations  15.1 us (6%)
  local copies, waits for them, and re-layouts  11.6 us (4%)
    psum x1, waiting for transfers between devices, shards(): summed_one, summed_two = lax.psum((partial_one, summed_two), ('gx', 'gy'))  118 us
    dot_general x27, matrix products, conv_pad(): jnp.einsum('co,cxyz->oxyz', folded[row_off, col_off], window, preferred_e...  26.6 us
    ppermute x6, starting transfers between devices, padded_2(): lax.ppermute(tail, axis, [(i, (i + 1) % count) for i in range(ends)])  24 us
    concatenate x3, other arithmetic, padded_2(): jnp.concatenate([lax.ppermute(tail, axis, [(i, (i + 1) % count) for i in...  11 us
    dot_general x9, matrix products, grad_forward(): jnp.einsum('cxyz,oxyz->co', window, grad, preferred_element_type=jnp.floa...  9.99 us
    dot_general x9, matrix products, grad_backward(): jnp.einsum('cxyz,kxyz->ck', activ, window, preferred_element_type=jnp.flo...  9.26 us
    concatenate x2, other arithmetic, stack_depth(): jnp.concatenate([padded[..., 0:depth], padded[..., 1:depth + 1], padded[....  9.24 us
    ppermute x6, starting transfers between devices, padded_2(): lax.ppermute(head, axis, [((i + 1) % count, i) for i in range(ends)])  8.17 us
  transfers between devices with their start and end apart: 13, of which 2 were waited for; matrix products, arithmetic and copies ran while one was open for 19% of the time, Pallas kernels for 0%

commit v1 on v0

v1 whole, which is shorter than its diff:
```python
import functools
import math

import jax
import jax.numpy as jnp
from jax import lax
from jax.experimental import pallas as pl
from jax.experimental.pallas import tpu as pltpu
from jax.sharding import PartitionSpec as P

BS = 8
MESH = pl.DeviceIdType.MESH
F32 = jnp.float32
BF16 = jnp.bfloat16
SCATTER = jnp.bfloat16
GATHER = jnp.float32
DIRS = ((-1, 0), (1, 0), (0, -1), (0, 1), (-1, -1), (-1, 1), (1, -1), (1, 1))


def upsample(block_mask):
    nbx, nby, nbz = block_mask.shape
    wide = jnp.broadcast_to(block_mask[:, None, :, None, :, None], (nbx, BS, nby, BS, nbz, BS))
    return wide.reshape(nbx * BS, nby * BS, nbz * BS)


def kernel(
    nx, ny, tx, ty, tz, ch, rows, scale,
    a_in, g_in, m_in, w1, w2, w3,
    out_f, out_one, out_two,
    s_a, s_g, s_h, acc, pre, act, pg,
    hx, hy, hc,
    part, part_s, rs, gyb, fin, tot,
    halo_send, halo_recv, rs_send, rs_recv, gy_send, gy_recv, ag_send, ag_recv,
):
    ix, iy = lax.axis_index("gx"), lax.axis_index("gy")
    width = ty * tz
    taps = 3 * ch

    def has(dx, dy):
        okay = None
        for pos, size, step in ((ix, nx, dx), (iy, ny, dy)):
            if step == 0:
                continue
            cond = (pos > 0) if step < 0 else (pos < size - 1)
            okay = cond if okay is None else jnp.logical_and(okay, cond)
        return okay

    barrier = pltpu.get_barrier_semaphore()
    for d in range(1, nx):
        pl.semaphore_signal(barrier, 1, device_id=(lax.rem(ix + d, nx), iy), device_id_type=MESH)
    for d in range(1, ny):
        pl.semaphore_signal(barrier, 1, device_id=(ix, lax.rem(iy + d, ny)), device_id_type=MESH)
    for dx, dy in DIRS[4:]:
        @pl.when(has(dx, dy))
        def _(dx=dx, dy=dy):
            pl.semaphore_signal(barrier, 1, device_id=(ix + dx, iy + dy), device_id_type=MESH)
    sides_x = jnp.where(ix > 0, 1, 0) + jnp.where(ix < nx - 1, 1, 0)
    sides_y = jnp.where(iy > 0, 1, 0) + jnp.where(iy < ny - 1, 1, 0)
    pl.semaphore_wait(barrier, nx + ny - 2 + sides_x * sides_y)

    def edge(source, arr, d, x0, y0):
        dx, dy = DIRS[d]
        xe = x0 if dx < 0 else x0 + tx - 1
        le = y0 * tz if dy < 0 else (y0 + ty - 1) * tz
        if dy == 0:
            src, dst = source.at[xe, :, pl.ds(y0 * tz, width)], hx.at[arr, d]
        elif dx == 0:
            src, dst = source.at[pl.ds(x0, tx), :, pl.ds(le, tz)], hy.at[arr, d - 2]
        else:
            src, dst = source.at[xe, :, pl.ds(le, tz)], hc.at[arr, d - 4]
        return pltpu.make_async_remote_copy(
            src_ref=src, dst_ref=dst,
            send_sem=halo_send.at[arr, d], recv_sem=halo_recv.at[arr, d],
            device_id=(ix + dx, iy + dy), device_id_type=MESH,
        )

    def send_halo(source, arr, x0, y0):
        for d in range(8):
            @pl.when(has(*DIRS[d]))
            def _(d=d):
                edge(source, arr, d, x0, y0).start()

    def sent_halo(source, arr, x0, y0):
        for d in range(8):
            @pl.when(has(*DIRS[d]))
            def _(d=d):
                edge(source, arr, d, x0, y0).wait_send()

    def put(stack, xp, yp, slab):
        zero = jnp.zeros((ch, 1), slab.dtype)
        at = pl.ds(yp * tz, tz)
        stack[xp, 0:ch, at] = jnp.concatenate([zero, slab[:, : tz - 1]], axis=1)
        stack[xp, ch : 2 * ch, at] = slab
        stack[xp, 2 * ch : taps, at] = jnp.concatenate([slab[:, 1:], zero], axis=1)

    def fill_inside(stack, source, x0, y0):
        def body(x, carry):
            for y in range(ty):
                put(stack, x + 1, y + 1, source[x + x0, :, (y + y0) * tz : (y + y0 + 1) * tz])
            return carry
        lax.fori_loop(0, tx, body, 0)

    def fill_halo(stack, source, arr, x0, y0):
        for d in range(8):
            dx, dy = DIRS[d]
            xp = tx + 1 if dx < 0 else 0
            yp = ty + 1 if dy < 0 else 0
            near = has(-dx, -dy)

            @pl.when(near)
            def _(d=d, dx=dx, dy=dy, xp=xp, yp=yp):
                edge(source, arr, d, x0, y0).wait_recv()
                if dy == 0:
                    for y in range(ty):
                        put(stack, xp, y + 1, hx[arr, d, :, y * tz : (y + 1) * tz])
                elif dx == 0:
                    def body(x, carry):
                        put(stack, x + 1, yp, hy[arr, d - 2, x])
                        return carry
                    lax.fori_loop(0, tx, body, 0)
                else:
                    put(stack, xp, yp, hc[arr, d - 4])

            @pl.when(jnp.logical_not(near))
            def _(dx=dx, dy=dy, xp=xp, yp=yp):
                if dy == 0:
                    stack[xp, :, pl.ds(tz, width)] = jnp.zeros((taps, width), BF16)
                elif dx == 0:
                    stack[1 : tx + 1, :, pl.ds(yp * tz, tz)] = jnp.zeros((tx, taps, tz), BF16)
                else:
                    stack[xp, :, pl.ds(yp * tz, tz)] = jnp.zeros((taps, tz), BF16)

    def conv(stack, weights, total, first, last):
        def body(xp, carry):
            window = jnp.concatenate(
                [stack[xp, :, j * tz : j * tz + width] for j in range(3)], axis=0
            )
            got = jnp.dot(weights[...], window, preferred_element_type=F32)
            for j in range(3):
                total[xp - j + 2] += got[j * ch : (j + 1) * ch]
            return carry
        lax.fori_loop(first, last, body, 0)

    def grad(local, stack, which):
        tot[...] = jnp.zeros_like(tot)

        def body(xp, carry):
            left = jnp.concatenate(
                [
                    local[xp - jx + 2, :, (2 - jy) * tz : (2 - jy + ty + 2) * tz]
                    for jx in range(3)
                    for jy in range(3)
                ],
                axis=0,
            )
            tot[...] += lax.dot_general(
                left, stack[xp], (((1,), (1,)), ((), ())), preferred_element_type=F32
            )
            return carry
        lax.fori_loop(0, tx + 2, body, 0)
        full = 9 * ch
        half = full // 2
        part[which, 0:full, :] = tot[:, 0 : 2 * ch]
        part[which, full : full + half, :] = jnp.concatenate(
            [tot[0:half, 2 * ch :], tot[half:full, 2 * ch :]], axis=1
        )
        part_s[which] = part[which].astype(SCATTER)

    def rs_copy(which, d):
        to = lax.rem(ix + d, nx)
        return pltpu.make_async_remote_copy(
            src_ref=part_s.at[which, pl.ds(to * rows, rows)], dst_ref=rs.at[which, d - 1],
            send_sem=rs_send.at[which, d - 1], recv_sem=rs_recv.at[which, d - 1],
            device_id=(to, iy), device_id_type=MESH,
        )

    def rs_start(which):
        for d in range(1, nx):
            rs_copy(which, d).start()

    def gy_copy(which, d):
        return pltpu.make_async_remote_copy(
            src_ref=gyb.at[which, iy], dst_ref=gyb.at[which, iy],
            send_sem=gy_send.at[which, d - 1], recv_sem=gy_recv.at[which, d - 1],
            device_id=(ix, lax.rem(iy + d, ny)), device_id_type=MESH,
        )

    def gy_wait(which, d):
        frm = lax.rem(iy + ny - d, ny)
        pltpu.make_async_remote_copy(
            src_ref=gyb.at[which, frm], dst_ref=gyb.at[which, frm],
            send_sem=gy_send.at[which, d - 1], recv_sem=gy_recv.at[which, d - 1],
            device_id=(ix, lax.rem(iy + d, ny)), device_id_type=MESH,
        ).wait_recv()

    def gy_start(which):
        for d in range(1, nx):
            rs_copy(which, d).wait_recv()
        total = part[which, pl.ds(pl.multiple_of(ix * rows, 8), rows)]
        for d in range(1, nx):
            total = total + rs[which, d - 1].astype(F32)
        gyb[which, iy] = total
        for d in range(1, ny):
            gy_copy(which, d).start()

    def ag_copy(which, d):
        return pltpu.make_async_remote_copy(
            src_ref=fin.at[which, ix], dst_ref=fin.at[which, ix],
            send_sem=ag_send.at[which, d - 1], recv_sem=ag_recv.at[which, d - 1],
            device_id=(lax.rem(ix + d, nx), iy), device_id_type=MESH,
        )

    def ag_wait(which, d):
        frm = lax.rem(ix + nx - d, nx)
        pltpu.make_async_remote_copy(
            src_ref=fin.at[which, frm], dst_ref=fin.at[which, frm],
            send_sem=ag_send.at[which, d - 1], recv_sem=ag_recv.at[which, d - 1],
            device_id=(lax.rem(ix + d, nx), iy), device_id_type=MESH,
        ).wait_recv()

    def ag_start(which):
        for d in range(1, ny):
            gy_wait(which, d)
        total = gyb[which, 0]
        for d in range(1, ny):
            total = total + gyb[which, d]
        fin[which, ix] = (total * scale).astype(GATHER)
        for d in range(1, nx):
            ag_copy(which, d).start()

    def finish(which, out):
        for d in range(1, nx):
            ag_wait(which, d)
        half = 9 * ch // 2
        flat = fin[which].astype(F32).reshape(nx * rows, 2 * ch)
        for j in range(9):
            block = flat[j * ch : (j + 1) * ch]
            lo = j * ch
            for k in range(2):
                emit(which, out, j, k, block[:, k * ch : (k + 1) * ch])
            if lo + ch <= half:
                tail = flat[9 * ch + lo : 9 * ch + lo + ch, 0:ch]
            elif lo >= half:
                tail = flat[9 * ch + lo - half : 9 * ch + lo - half + ch, ch:]
            else:
                cut = half - lo
                tail = jnp.concatenate(
                    [flat[9 * ch + lo : 9 * ch + half, 0:ch], flat[9 * ch : 10 * ch - cut, ch:]], axis=0
                )
            emit(which, out, j, 2, tail)

    def emit(which, out, j, k, block):
        jx, jy = j // 3, j % 3
        if which == 0:
            out[2 - jx, 2 - jy, 2 - k] = block
        else:
            out[jx, jy, k] = jnp.transpose(block)

    send_halo(a_in, 0, 0, 0)
    send_halo(g_in, 1, 0, 0)

    for pad in (act, pg):
        for x in (0, 1, tx + 2, tx + 3):
            pad[x] = jnp.zeros(pad.shape[1:], BF16)
        pad[:, :, 0 : 2 * tz] = jnp.zeros((tx + 4, ch, 2 * tz), BF16)
        pad[:, :, 2 * tz + width :] = jnp.zeros((tx + 4, ch, 2 * tz), BF16)
    part[:, 27 * ch // 2 :, :] = jnp.zeros((2, nx * rows - 27 * ch // 2, 2 * ch), F32)
    pre[...] = jnp.zeros_like(pre)
    acc[...] = jnp.zeros_like(acc)

    fill_inside(s_a, a_in, 0, 0)
    fill_inside(s_g, g_in, 0, 0)
    fill_halo(s_a, a_in, 0, 0, 0)
    conv(s_a, w1, pre, 0, tx + 2)
    fill_halo(s_g, g_in, 1, 0, 0)
    conv(s_g, w2, acc, 0, tx + 2)

    def middle(x, carry):
        value = pre[x + 2]
        mask = m_in[x]
        sig = jax.nn.sigmoid(value)
        act[x + 2, :, 2 * tz : 2 * tz + width] = (mask * (value * sig)).astype(BF16)
        slope = sig * (1.0 + value * (1.0 - sig))
        pg[x + 2, :, 2 * tz : 2 * tz + width] = (mask * slope * acc[x + 2]).astype(BF16)
        return carry
    lax.fori_loop(0, tx, middle, 0)
    send_halo(pg, 2, 2, 2)
    grad(act, s_g, 0)
    rs_start(0)
    grad(pg, s_a, 1)
    rs_start(1)
    acc[...] = jnp.zeros_like(acc)
    fill_inside(s_h, pg, 2, 2)
    gy_start(0)
    fill_halo(s_h, pg, 2, 2, 2)
    mid = (tx + 2) // 2
    conv(s_h, w3, acc, 0, mid)
    gy_start(1)
    ag_start(0)
    conv(s_h, w3, acc, mid, tx + 2)
    ag_start(1)

    def ending(x, carry):
        out_f[x] = (g_in[x].astype(F32) + m_in[x] * acc[x + 2]).astype(BF16)
        return carry
    lax.fori_loop(0, tx, ending, 0)
    finish(0, out_two)
    finish(1, out_one)
    sent_halo(a_in, 0, 0, 0)
    sent_halo(g_in, 1, 0, 0)
    sent_halo(pg, 2, 2, 2)
    for which in range(2):
        for d in range(1, nx):
            rs_copy(which, d).wait_send()
            ag_copy(which, d).wait_send()
        for d in range(1, ny):
            gy_copy(which, d).wait_send()


def shards(features, cotangent, block_mask, kernel_one, kernel_two):
    ch, tx, ty, tz = features.shape
    nx, ny = lax.axis_size("gx"), lax.axis_size("gy")
    width = ty * tz
    cell = upsample(block_mask)
    cell_b = cell.astype(BF16)[None]
    a_in = jnp.transpose(features * cell_b, (1, 0, 2, 3)).reshape(tx, ch, width)
    g_in = jnp.transpose(cotangent * cell_b, (1, 0, 2, 3)).reshape(tx, ch, width)
    m_in = cell.astype(F32).reshape(tx, 1, width)
    w1 = jnp.transpose(kernel_one, (0, 4, 1, 2, 3)).reshape(3 * ch, 9 * ch)
    w2 = jnp.transpose(jnp.flip(kernel_two, (0, 1, 2)), (0, 3, 1, 2, 4)).reshape(3 * ch, 9 * ch)
    w3 = jnp.transpose(jnp.flip(kernel_one, (0, 1, 2)), (0, 3, 1, 2, 4)).reshape(3 * ch, 9 * ch)
    need = -(-(27 * ch // 2) // nx)
    rows = -(-need // 16) * 16
    scale = 1.0 / math.sqrt(tx * ty * tz * nx * ny)
    vm = pl.BlockSpec(memory_space=pltpu.VMEM)
    dma = pltpu.SemaphoreType.DMA
    stack = pltpu.VMEM((tx + 2, 3 * ch, (ty + 2) * tz), BF16)
    total = pltpu.VMEM((tx + 4, ch, width), F32)
    pad = pltpu.VMEM((tx + 4, ch, (ty + 4) * tz), BF16)
    out_f, out_one, out_two = pl.pallas_call(
        functools.partial(kernel, nx, ny, tx, ty, tz, ch, rows, scale),
        out_shape=(
            jax.ShapeDtypeStruct((tx, ch, width), BF16),
            jax.ShapeDtypeStruct((3, 3, 3, ch, ch), F32),
            jax.ShapeDtypeStruct((3, 3, 3, ch, ch), F32),
        ),
        in_specs=[vm] * 6,
        out_specs=(vm, vm, vm),
        scratch_shapes=[
            stack, stack, stack, total, total, pad, pad,
            pltpu.VMEM((3, 2, ch, width), BF16),
            pltpu.VMEM((3, 2, tx, ch, tz), BF16),
            pltpu.VMEM((3, 4, ch, tz), BF16),
            pltpu.VMEM((2, nx * rows, 2 * ch), F32),
            pltpu.VMEM((2, nx * rows, 2 * ch), SCATTER),
            pltpu.VMEM((2, nx - 1, rows, 2 * ch), SCATTER),
            pltpu.VMEM((2, ny, rows, 2 * ch), F32),
            pltpu.VMEM((2, nx, rows, 2 * ch), GATHER),
            pltpu.VMEM((9 * ch, 3 * ch), F32),
            dma((3, 8)), dma((3, 8)),
            dma((2, nx - 1)), dma((2, nx - 1)),
            dma((2, ny - 1)), dma((2, ny - 1)),
            dma((2, nx - 1)), dma((2, nx - 1)),
        ],
        compiler_params=pltpu.CompilerParams(
            collective_id=0, has_side_effects=True, vmem_limit_bytes=56 * 2**20
        ),
    )(a_in, g_in, m_in, w1, w2, w3)
    grad_features = jnp.transpose(out_f.reshape(tx, ch, ty, tz), (1, 0, 2, 3))
    return (grad_features, out_one, out_two)


def solution(mesh):
    placed = (P(None, "gx", "gy", None), P(None, "gx", "gy", None), P("gx", "gy", None), P(), P())
    return jax.shard_map(
        shards,
        mesh=mesh,
        in_specs=placed,
        out_specs=(P(None, "gx", "gy", None), P(), P()),
        check_vma=False,
    )
```

time: 265 us -> 80.3 us (0.30)
  the two profiles are of different devices: /device:TPU:0 before, /device:TPU:27 now
where the time goes in v1:
time: 80.3 us; the launch traced here: 80 us
  Pallas kernels  61 us (76%)
  local copies, waits for them, and re-layouts  16.9 us (21%)
  other arithmetic  1.37 us (2%)
    pallas_call x1, Pallas kernels, shards(): pl.pallas_call(functools.partial(kernel, nx, ny, tx, ty, tz, ch, rows, sc...  61 us
    unnamed x13, local copies, waits for them, and re-layouts  4.55 us
    reshape x2, local copies, waits for them, and re-layouts, shards(): jnp.transpose(cotangent * cell_b, (1, 0, 2, 3)).reshape(tx, ch, width)  2.04 us
    reshape x2, local copies, waits for them, and re-layouts, shards(): a_in = jnp.transpose(features * cell_b, (1, 0, 2, 3)).reshape(tx, ch, width)  2.02 us

profile of v1, /device:TPU:27, one launch (start us, length us, event | category | flops | bytes accessed | tf_op | source)
XLA Modules:
  0.0 80.0 jit_solution(6939784081344517915)
XLA Ops:
  0.6 0.0 copy-start.4
  0.6 0.6 copy-done.4
  1.3 0.1 broadcast_in_dim.11
  1.4 0.1 convert_element_type.26
  1.5 0.1 broadcast_in_dim.12
  1.5 0.1 convert_element_type.29
  1.6 0.6 broadcast_in_dim.13.m_in
  2.3 1.0 %reverse_bitcast_fusion.1 = bf16[3,64,3,3,64]{4,1,3,2,0:T(8,128)(2,1)S(1)} fusion(bf16[3,3,3,64,64]{4,3,2,1,0:T(8,128)(2,1)} %param.9), kind=kLoop, calls=%fused_computation.4 | loop fusion | bytes 442368 | tf_op jit(solution)/shard_map/transpose | solution.py:330
  3.3 0.4 copy.17
  3.7 0.0 copy-start
  3.7 1.1 %reshape.40.w2 = bf16[192,576]{1,0:T(8,128)(2,1)} reshape(bf16[3,64,3,3,64]{4,3,2,1,0:T(4,128)(2,1)S(1)} %copy.17) | data formatting | bytes 442368 | tf_op jit(solution)/shard_map/reshape | solution.py:330
  4.8 0.0 copy-done
  4.8 0.4 copy.18
  5.2 1.1 %reshape.41.w3 = bf16[192,576]{1,0:T(8,128)(2,1)} reshape(bf16[3,64,3,3,64]{4,3,2,1,0:T(4,128)(2,1)S(1)} %copy.18) | data formatting | bytes 442368 | tf_op jit(solution)/shard_map/reshape | solution.py:331
  6.3 0.0 copy-start.1
  6.3 0.9 %copy.16 = bf16[3,64,3,3,64]{4,3,2,1,0:T(4,128)(2,1)S(1)} copy(bf16[3,64,3,3,64]{1,4,3,2,0:T(8,128)(2,1)S(1)} %bitcast.32) | data formatting | bytes 442368 | tf_op jit(solution)/shard_map/transpose | solution.py:329
  7.3 1.1 %reshape.39.w1 = bf16[192,576]{1,0:T(8,128)(2,1)} reshape(bf16[3,64,3,3,64]{4,3,2,1,0:T(4,128)(2,1)S(1)} %copy.16) | data formatting | bytes 442368 | tf_op jit(solution)/shard_map/reshape | solution.py:329
  8.4 0.0 copy-done.1
  8.4 1.4 %multiply_bitcast_fusion = (bf16[8,64,8,128]{3,2,0,1:T(8,128)(2,1)S(1)}, bf16[8,64,8,128]{3,2,0,1:T(8,128)(2,1)S(1)}) fusion(bf16[64,8,8,128]{3,2,1,0:T(8,128)(2,1)S(1)} %copy-done.1, bf16[128]{0:T(256)(128)(2,1)S(1)} %convert_element_type.26, bf16[64,8,8,128]{3,2,1,0:T(8,128)(2,1)} %param.5), kind=kLoop, calls=%fused_computation.1 | loop fusion | flops 1048576 | bytes 4194560 | tf_op jit(solution)/shard_map/transpose | solution.py:327
  9.7 0.5 reshape.44
  10.2 1.5 %copy.21.g_in = bf16[8,64,1024]{2,1,0:T(8,128)(2,1)} copy(bf16[8,64,1024]{2,0,1:T(8,128)(2,1)S(1)} %reshape.44) | data formatting | bytes 2097152 | tf_op jit(solution)/shard_map/reshape | solution.py:327
  11.8 0.5 reshape.43
  12.3 1.5 %copy.20.a_in = bf16[8,64,1024]{2,1,0:T(8,128)(2,1)} copy(bf16[8,64,1024]{2,0,1:T(8,128)(2,1)S(1)} %reshape.43) | data formatting | bytes 2097152 | tf_op jit(solution)/shard_map/reshape | solution.py:326
  13.8 61.0 %shard_map.76 = (bf16[8,64,1024]{2,1,0:T(8,128)(2,1)}, f32[3,3,3,64,64]{4,3,2,1,0:T(8,128)}, f32[3,3,3,64,64]{4,3,2,1,0:T(8,128)}) custom-call(bf16[8,64,1024]{2,1,0:T(8,128)(2,1)} %copy.20.a_in, bf16[8,64,1024]{2,1,0:T(8,128)(2,1)} %copy.21.g_in, f32[8,1,1024]{2,1,0:T(1,128)} %broadcast_in_dim.13.m_in, bf16[192,576]{1,0:T(8,128)(2,1)} %reshape.39.w1, ...), custom_call_target="tpu_custom_call" | custom-call | tf_op jit(solution)/shard_map/pallas_call | solution.py:340
  74.8 1.5 %copy.22 = bf16[64,8,8,128]{3,2,1,0:T(8,128)(2,1)S(1)} copy(bf16[64,8,8,128]{3,1,2,0:T(8,128)(2,1)} %bitcast.33) | data formatting | bytes 2097152
  76.3 0.0 copy-start.3
  76.3 1.3 %copy_bitcast_fusion = bf16[64,8,8,128]{3,2,1,0:T(8,128)(2,1)} fusion(bf16[8,64,8,128]{3,2,1,0:T(8,128)(2,1)S(1)} %bitcast.31), kind=kLoop, calls=%fused_computation | loop fusion | bytes 2097152 | tf_op jit(solution)/shard_map/transpose | solution.py:369
  77.6 0.0 copy-done.3
  77.6 0.0 copy-start.2
  77.6 0.9 %copy.26 = f32[3,3,3,64,64]{4,3,2,1,0:T(8,128)} copy(f32[3,3,3,64,64]{4,3,2,1,0:T(8,128)S(1)} %copy-done.3) | data formatting | bytes 884736
  78.5 0.6 copy-done.2
  79.0 0.9 %copy.27 = f32[3,3,3,64,64]{4,3,2,1,0:T(8,128)} copy(f32[3,3,3,64,64]{4,3,2,1,0:T(8,128)S(1)} %copy-done.2) | data formatting | bytes 884736
  (2 shorter events, 0.0 us)
Async XLA Ops:
  0.6 0.7 copy-start.4
  3.7 1.1 %copy-start = (bf16[3,3,3,64,64]{4,3,2,1,0:T(8,128)(2,1)S(1)}, bf16[3,3,3,64,64]{4,3,2,1,0:T(8,128)(2,1)}, u32[]{:S(2)}) copy-start(bf16[3,3,3,64,64]{4,3,2,1,0:T(8,128)(2,1)} %param.8) | copy-start | bytes 663556
  6.3 2.0 %copy-start.1 = (bf16[64,8,8,128]{3,2,1,0:T(8,128)(2,1)S(1)}, bf16[64,8,8,128]{3,2,1,0:T(8,128)(2,1)}, u32[]{:S(2)}) copy-start(bf16[64,8,8,128]{3,2,1,0:T(8,128)(2,1)} %param.6) | copy-start | bytes 3145732
  76.3 1.3 %copy-start.3 = (f32[3,3,3,64,64]{4,3,2,1,0:T(8,128)S(1)}, f32[3,3,3,64,64]{4,3,2,1,0:T(8,128)}, u32[]{:S(2)}) copy-start(f32[3,3,3,64,64]{4,3,2,1,0:T(8,128)} %get-tuple-element.17) | copy-start | bytes 1327108
  77.6 1.5 %copy-start.2 = (f32[3,3,3,64,64]{4,3,2,1,0:T(8,128)S(1)}, f32[3,3,3,64,64]{4,3,2,1,0:T(8,128)}, u32[]{:S(2)}) copy-start(f32[3,3,3,64,64]{4,3,2,1,0:T(8,128)} %get-tuple-element.18) | copy-start | bytes 1327108

commit v2 on v1

--- a/solution.py
+++ b/solution.py
@@ -13,7 +13,7 @@
 F32 = jnp.float32
 BF16 = jnp.bfloat16
 SCATTER = jnp.bfloat16
-GATHER = jnp.float32
+GATHER = jnp.bfloat16
 DIRS = ((-1, 0), (1, 0), (0, -1), (0, 1), (-1, -1), (-1, 1), (1, -1), (1, 1))
 
 
@@ -25,11 +25,11 @@
 
 def kernel(
     nx, ny, tx, ty, tz, ch, rows, scale,
-    a_in, g_in, m_in, w1, w2, w3,
+    a_in, g_in, m_in, k1, k2,
     out_f, out_one, out_two,
     s_a, s_g, s_h, acc, pre, act, pg,
     hx, hy, hc,
-    part, part_s, rs, gyb, fin, tot,
+    part, part_s, rs, csum, gsl, fin, tot, w1, w2, w3,
     halo_send, halo_recv, rs_send, rs_recv, gy_send, gy_recv, ag_send, ag_recv,
 ):
     ix, iy = lax.axis_index("gx"), lax.axis_index("gy")
@@ -178,30 +178,44 @@
         for d in range(1, nx):
             rs_copy(which, d).start()
 
-    def gy_copy(which, d):
+    sub = rows // ny
+
+    def gs_copy(which, d):
+        to = lax.rem(iy + d, ny)
         return pltpu.make_async_remote_copy(
-            src_ref=gyb.at[which, iy], dst_ref=gyb.at[which, iy],
+            src_ref=csum.at[which, pl.ds(to * sub, sub)], dst_ref=gsl.at[which, d - 1],
             send_sem=gy_send.at[which, d - 1], recv_sem=gy_recv.at[which, d - 1],
+            device_id=(ix, to), device_id_type=MESH,
+        )
+
+    def gg_copy(which, d, owner):
+        mine = fin.at[which, ix, pl.ds(owner * sub, sub)]
+        return pltpu.make_async_remote_copy(
+            src_ref=mine, dst_ref=mine,
+            send_sem=gy_send.at[which + 2, d - 1], recv_sem=gy_recv.at[which + 2, d - 1],
             device_id=(ix, lax.rem(iy + d, ny)), device_id_type=MESH,
         )
 
-    def gy_wait(which, d):
-        frm = lax.rem(iy + ny - d, ny)
-        pltpu.make_async_remote_copy(
-            src_ref=gyb.at[which, frm], dst_ref=gyb.at[which, frm],
-            send_sem=gy_send.at[which, d - 1], recv_sem=gy_recv.at[which, d - 1],
-            device_id=(ix, lax.rem(iy + d, ny)), device_id_type=MESH,
-        ).wait_recv()
-
-    def gy_start(which):
+    def gs_start(which):
         for d in range(1, nx):
             rs_copy(which, d).wait_recv()
-        total = part[which, pl.ds(pl.multiple_of(ix * rows, 8), rows)]
+        total = part[which, pl.ds(pl.multiple_of(ix * rows, 16), rows)]
         for d in range(1, nx):
             total = total + rs[which, d - 1].astype(F32)
-        gyb[which, iy] = total
-        for d in range(1, ny):
-            gy_copy(which, d).start()
+        csum[which] = total
+        for d in range(1, ny):
+            gs_copy(which, d).start()
+
+    def gg_start(which):
+        for d in range(1, ny):
+            gs_copy(which, d).wait_recv()
+        at = pl.ds(pl.multiple_of(iy * sub, 16), sub)
+        total = csum[which, at]
+        for d in range(1, ny):
+            total = total + gsl[which, d - 1]
+        fin[which, ix, at] = (total * scale).astype(GATHER)
+        for d in range(1, ny):
+            gg_copy(which, d, iy).start()
 
     def ag_copy(which, d):
         return pltpu.make_async_remote_copy(
@@ -220,11 +234,7 @@
 
     def ag_start(which):
         for d in range(1, ny):
-            gy_wait(which, d)
-        total = gyb[which, 0]
-        for d in range(1, ny):
-            total = total + gyb[which, d]
-        fin[which, ix] = (total * scale).astype(GATHER)
+            gg_copy(which, d, lax.rem(iy + ny - d, ny)).wait_recv()
         for d in range(1, nx):
             ag_copy(which, d).start()
 
@@ -268,36 +278,52 @@
     pre[...] = jnp.zeros_like(pre)
     acc[...] = jnp.zeros_like(acc)
 
+    for jx in range(3):
+        low = jx * ch
+        for n in range(0, 9, 2):
+            these = [jx * 9 + m for m in range(n, min(n + 2, 9))]
+            cols = slice(n * ch, (n + len(these)) * ch)
+            w1[low : low + ch, cols] = jnp.transpose(jnp.concatenate([k1[t] for t in these], axis=0))
+            w2[low : low + ch, cols] = jnp.concatenate([k2[26 - t] for t in these], axis=1)
+            w3[low : low + ch, cols] = jnp.concatenate([k1[26 - t] for t in these], axis=1)
+
     fill_inside(s_a, a_in, 0, 0)
     fill_inside(s_g, g_in, 0, 0)
     fill_halo(s_a, a_in, 0, 0, 0)
     conv(s_a, w1, pre, 0, tx + 2)
-    fill_halo(s_g, g_in, 1, 0, 0)
-    conv(s_g, w2, acc, 0, tx + 2)
 
     def middle(x, carry):
         value = pre[x + 2]
         mask = m_in[x]
         sig = jax.nn.sigmoid(value)
         act[x + 2, :, 2 * tz : 2 * tz + width] = (mask * (value * sig)).astype(BF16)
-        slope = sig * (1.0 + value * (1.0 - sig))
-        pg[x + 2, :, 2 * tz : 2 * tz + width] = (mask * slope * acc[x + 2]).astype(BF16)
+        pre[x + 2] = mask * (sig * (1.0 + value * (1.0 - sig)))
         return carry
     lax.fori_loop(0, tx, middle, 0)
-    send_halo(pg, 2, 2, 2)
+    fill_halo(s_g, g_in, 1, 0, 0)
     grad(act, s_g, 0)
     rs_start(0)
+    conv(s_g, w2, acc, 0, tx + 2)
+
+    def after(x, carry):
+        pg[x + 2, :, 2 * tz : 2 * tz + width] = (pre[x + 2] * acc[x + 2]).astype(BF16)
+        return carry
+    lax.fori_loop(0, tx, after, 0)
+    send_halo(pg, 2, 2, 2)
+    gs_start(0)
     grad(pg, s_a, 1)
     rs_start(1)
+    gg_start(0)
     acc[...] = jnp.zeros_like(acc)
     fill_inside(s_h, pg, 2, 2)
-    gy_start(0)
+    ag_start(0)
     fill_halo(s_h, pg, 2, 2, 2)
-    mid = (tx + 2) // 2
-    conv(s_h, w3, acc, 0, mid)
-    gy_start(1)
-    ag_start(0)
-    conv(s_h, w3, acc, mid, tx + 2)
+    cuts = [(tx + 2) * k // 5 for k in (0, 2, 4, 5)]
+    conv(s_h, w3, acc, cuts[0], cuts[1])
+    gs_start(1)
+    conv(s_h, w3, acc, cuts[1], cuts[2])
+    gg_start(1)
+    conv(s_h, w3, acc, cuts[2], cuts[3])
     ag_start(1)
 
     def ending(x, carry):
@@ -314,7 +340,8 @@
             rs_copy(which, d).wait_send()
             ag_copy(which, d).wait_send()
         for d in range(1, ny):
-            gy_copy(which, d).wait_send()
+            gs_copy(which, d).wait_send()
+            gg_copy(which, d, iy).wait_send()
 
 
 def shards(features, cotangent, block_mask, kernel_one, kernel_two):
@@ -326,12 +353,13 @@
     a_in = jnp.transpose(features * cell_b, (1, 0, 2, 3)).reshape(tx, ch, width)
     g_in = jnp.transpose(cotangent * cell_b, (1, 0, 2, 3)).reshape(tx, ch, width)
     m_in = cell.astype(F32).reshape(tx, 1, width)
-    w1 = jnp.transpose(kernel_one, (0, 4, 1, 2, 3)).reshape(3 * ch, 9 * ch)
-    w2 = jnp.transpose(jnp.flip(kernel_two, (0, 1, 2)), (0, 3, 1, 2, 4)).reshape(3 * ch, 9 * ch)
-    w3 = jnp.transpose(jnp.flip(kernel_one, (0, 1, 2)), (0, 3, 1, 2, 4)).reshape(3 * ch, 9 * ch)
+    k1 = kernel_one.reshape(27, ch, ch)
+    k2 = kernel_two.reshape(27, ch, ch)
     need = -(-(27 * ch // 2) // nx)
-    rows = -(-need // 16) * 16
+    rows = -(-need // (16 * ny)) * 16 * ny
+    sub = rows // ny
     scale = 1.0 / math.sqrt(tx * ty * tz * nx * ny)
+    weight = pltpu.VMEM((3 * ch, 9 * ch), BF16)
     vm = pl.BlockSpec(memory_space=pltpu.VMEM)
     dma = pltpu.SemaphoreType.DMA
     stack = pltpu.VMEM((tx + 2, 3 * ch, (ty + 2) * tz), BF16)
@@ -344,7 +372,7 @@
             jax.ShapeDtypeStruct((3, 3, 3, ch, ch), F32),
             jax.ShapeDtypeStruct((3, 3, 3, ch, ch), F32),
         ),
-        in_specs=[vm] * 6,
+        in_specs=[vm] * 5,
         out_specs=(vm, vm, vm),
         scratch_shapes=[
             stack, stack, stack, total, total, pad, pad,
@@ -354,18 +382,20 @@
             pltpu.VMEM((2, nx * rows, 2 * ch), F32),
             pltpu.VMEM((2, nx * rows, 2 * ch), SCATTER),
             pltpu.VMEM((2, nx - 1, rows, 2 * ch), SCATTER),
-            pltpu.VMEM((2, ny, rows, 2 * ch), F32),
+            pltpu.VMEM((2, rows, 2 * ch), F32),
+            pltpu.VMEM((2, ny - 1, sub, 2 * ch), F32),
             pltpu.VMEM((2, nx, rows, 2 * ch), GATHER),
             pltpu.VMEM((9 * ch, 3 * ch), F32),
+            weight, weight, weight,
             dma((3, 8)), dma((3, 8)),
             dma((2, nx - 1)), dma((2, nx - 1)),
-            dma((2, ny - 1)), dma((2, ny - 1)),
+            dma((4, ny - 1)), dma((4, ny - 1)),
             dma((2, nx - 1)), dma((2, nx - 1)),
         ],
         compiler_params=pltpu.CompilerParams(
             collective_id=0, has_side_effects=True, vmem_limit_bytes=56 * 2**20
         ),
-    )(a_in, g_in, m_in, w1, w2, w3)
+    )(a_in, g_in, m_in, k1, k2)
     grad_features = jnp.transpose(out_f.reshape(tx, ch, ty, tz), (1, 0, 2, 3))
     return (grad_features, out_one, out_two)
 

time: 80.3 us -> 74.4 us (0.927)
  the two profiles are of different devices: /device:TPU:27 before, /device:TPU:0 now
where the time goes in v2:
time: 74.4 us; the launch traced here: 74.2 us
  Pallas kernels  60.9 us (82%)
  local copies, waits for them, and re-layouts  10.8 us (15%)
  other arithmetic  1.68 us (2%)
    pallas_call x1, Pallas kernels, shards(): pl.pallas_call(functools.partial(kernel, nx, ny, tx, ty, tz, ch, rows, sc...  60.9 us
    unnamed x9, local copies, waits for them, and re-layouts  4.54 us
    reshape x2, local copies, waits for them, and re-layouts, shards(): jnp.transpose(cotangent * cell_b, (1, 0, 2, 3)).reshape(tx, ch, width)  2.05 us
    reshape x2, local copies, waits for them, and re-layouts, shards(): a_in = jnp.transpose(features * cell_b, (1, 0, 2, 3)).reshape(tx, ch, width)  2.02 us
    transpose x1, other arithmetic, shards(): jnp.transpose(cotangent * cell_b, (1, 0, 2, 3)).reshape(tx, ch, width)  1.68 us

profile of v2, /device:TPU:0, one launch (start us, length us, event | category | flops | bytes accessed | tf_op | source)
XLA Modules:
  0.0 74.2 jit_solution(5670669260994051402)
XLA Ops:
  0.6 0.0 copy-start.2
  0.6 0.6 copy-done.2
  1.3 0.1 broadcast_in_dim.11
  1.4 0.1 convert_element_type.26
  1.5 0.1 broadcast_in_dim.12
  1.5 0.1 convert_element_type.29
  1.6 0.6 broadcast_in_dim.13.m_in
  2.3 1.7 %multiply_bitcast_fusion = (bf16[8,64,8,128]{3,2,0,1:T(8,128)(2,1)S(1)}, bf16[8,64,8,128]{3,2,0,1:T(8,128)(2,1)S(1)}) fusion(bf16[64,8,8,128]{3,2,1,0:T(8,128)(2,1)} %param.6, bf16[128]{0:T(256)(128)(2,1)S(1)} %convert_element_type.26, bf16[64,8,8,128]{3,2,1,0:T(8,128)(2,1)} %param.5), kind=kLoop, calls=%fused_computation.1 | loop fusion | flops 1048576 | bytes 4194560 | tf_op jit(solution)/shard_map/transpose | solution.py:354
  4.0 0.5 reshape.40
  4.5 1.6 %copy.15.g_in = bf16[8,64,1024]{2,1,0:T(8,128)(2,1)} copy(bf16[8,64,1024]{2,0,1:T(8,128)(2,1)S(1)} %reshape.40) | data formatting | bytes 2097152 | tf_op jit(solution)/shard_map/reshape | solution.py:354
  6.0 0.5 reshape.39
  6.5 1.5 %copy.14.a_in = bf16[8,64,1024]{2,1,0:T(8,128)(2,1)} copy(bf16[8,64,1024]{2,0,1:T(8,128)(2,1)S(1)} %reshape.39) | data formatting | bytes 2097152 | tf_op jit(solution)/shard_map/reshape | solution.py:353
  8.0 60.9 %shard_map.76 = (bf16[8,64,1024]{2,1,0:T(8,128)(2,1)}, f32[3,3,3,64,64]{4,3,2,1,0:T(8,128)}, f32[3,3,3,64,64]{4,3,2,1,0:T(8,128)}) custom-call(bf16[8,64,1024]{2,1,0:T(8,128)(2,1)} %copy.14.a_in, bf16[8,64,1024]{2,1,0:T(8,128)(2,1)} %copy.15.g_in, f32[8,1,1024]{2,1,0:T(1,128)} %broadcast_in_dim.13.m_in, bf16[27,64,64]{2,1,0:T(8,128)(2,1)} %bitcast.30, ...), custom_call_target="tpu_custom_call" | custom-call | tf_op jit(solution)/shard_map/pallas_call | solution.py:368
  69.0 1.5 %copy.16 = bf16[64,8,8,128]{3,2,1,0:T(8,128)(2,1)S(1)} copy(bf16[64,8,8,128]{3,1,2,0:T(8,128)(2,1)} %bitcast.29) | data formatting | bytes 2097152
  70.5 0.0 copy-start.1
  70.5 1.3 %copy_bitcast_fusion = bf16[64,8,8,128]{3,2,1,0:T(8,128)(2,1)} fusion(bf16[8,64,8,128]{3,2,1,0:T(8,128)(2,1)S(1)} %bitcast.28), kind=kLoop, calls=%fused_computation | loop fusion | bytes 2097152 | tf_op jit(solution)/shard_map/transpose | solution.py:399
  71.8 0.0 copy-done.1
  71.8 0.0 copy-start
  71.8 0.9 %copy.20 = f32[3,3,3,64,64]{4,3,2,1,0:T(8,128)} copy(f32[3,3,3,64,64]{4,3,2,1,0:T(8,128)S(1)} %copy-done.1) | data formatting | bytes 884736
  72.7 0.6 copy-done
  73.2 0.9 %copy.21 = f32[3,3,3,64,64]{4,3,2,1,0:T(8,128)} copy(f32[3,3,3,64,64]{4,3,2,1,0:T(8,128)S(1)} %copy-done) | data formatting | bytes 884736
  (1 shorter events, 0.0 us)
Async XLA Ops:
  0.6 0.7 copy-start.2
  70.5 1.3 %copy-start.1 = (f32[3,3,3,64,64]{4,3,2,1,0:T(8,128)S(1)}, f32[3,3,3,64,64]{4,3,2,1,0:T(8,128)}, u32[]{:S(2)}) copy-start(f32[3,3,3,64,64]{4,3,2,1,0:T(8,128)} %get-tuple-element.17) | copy-start | bytes 1327108
  71.8 1.5 %copy-start = (f32[3,3,3,64,64]{4,3,2,1,0:T(8,128)S(1)}, f32[3,3,3,64,64]{4,3,2,1,0:T(8,128)}, u32[]{:S(2)}) copy-start(f32[3,3,3,64,64]{4,3,2,1,0:T(8,128)} %get-tuple-element.18) | copy-start | bytes 1327108
